TPU v7x, 256 devices: a whole 4x4x8 slice. The times are simulated.
256 devices in a mesh: tm: 32 (over x, y, z_hi), mp: 8 (over z_lo, core).
Axes of the slice: x: 4, y: 4, z: 8 (z_hi: 2, z_lo: 4; z = z_hi * 4 + z_lo), core: 2. Of those that a mesh axis runs over, the one named last changes fastest.
Arguments:
- frames: bfloat16 [4, 20480, 1024], P(None, 'tm'), may hold values from -8 to 8
- valid: int32 [4], replicated, may hold values from 5120 to 20480, as said below
- ln1_gain: float32 [1024], replicated, may hold values from 0.5 to 4
- w_query: bfloat16 [1024, 1024], P(None, 'mp'), may hold values from -0.1875 to 0.1875
- w_key: bfloat16 [1024, 1024], P(None, 'mp'), may hold values from -0.1875 to 0.1875
- w_value: bfloat16 [1024, 1024], P(None, 'mp'), may hold values from -0.1875 to 0.1875
- w_out: bfloat16 [1024, 1024], P('mp'), may hold values from -0.1875 to 0.1875
- ln2_gain: float32 [1024], replicated, may hold values from 0.5 to 4
- w_up: bfloat16 [1024, 4096], P(None, 'mp'), may hold values from -0.1875 to 0.1875
- w_down: bfloat16 [4096, 1024], P('mp'), may hold values from -0.09375 to 0.09375
Outputs:
- layer_out: bfloat16 [4, 20480, 1024], P(None, 'tm', 'mp')
Inputs may be any that keep to these rules, and one draw needn't show every extreme that they name: `valid`: live frames of each recording; recording 0 is complete.
All inputs are finite; a program needn't handle non-finite values.
Results may differ from a plain program's by a relative error of at most 0.027.
Values may be sent and summed in bfloat16 or wider, within the bound.
A program may use at most 128 MiB of HBM per device.

v0:
```python
import jax
import jax.numpy as jnp
from jax import lax
from jax.experimental import pallas as pl
from jax.experimental.pallas import tpu as pltpu
from jax.sharding import PartitionSpec as P

MESH = pl.DeviceIdType.MESH
F32 = jnp.float32
BF16 = jnp.bfloat16

D = 1024
SEG = 160
LOOK = 32
KEYS = SEG + LOOK
OWN = 2 * SEG
ROWS = OWN + LOOK
EXT = ROWS + 16
SLOTS = 128
EPS = 1e-05
NEG = -1e30
N_SEM = 208


def dot(a, b):
    return jnp.dot(a, b, preferred_element_type=F32)


def dot_t(a, b):
    return lax.dot_general(a, b, (((1,), (1,)), ((), ())), preferred_element_type=F32)


def normalize(x, gain):
    mean = jnp.sum(x, -1, keepdims=True) * (1.0 / D)
    square = jnp.sum(x * x, -1, keepdims=True) * (1.0 / D)
    return (x - mean) * lax.rsqrt(square - mean * mean + EPS) * gain


def kernel(
    valid, g1, g2, frames, wq, wk, wv, wo, up, dn, out,
    xs, nrm, qb, kb, vb, wq_b, wk_b, wv_b, wo_b, up_b, dn_b,
    mrow, mem_b, memf, bk, bv, fo, mixed, n2, hid, ob,
    loc_sem, send_sem, recv_sem,
):
    tm = lax.axis_index("tm")
    mp = lax.axis_index("mp")
    x = tm // 8
    y = (tm // 2) % 4
    zl = mp // 2
    z = (tm % 2) * 4 + zl
    c = mp % 2
    rec = zl

    def dev(px, py, pz, pc):
        return ((px * 4 + py) * 2 + pz // 4, (pz % 4) * 2 + pc)

    def z_dev(step):
        return dev(x, y, (z + step + 8) % 8, c)

    sibling = (tm, zl * 2 + 1 - c)

    used = [0]
    sent = []

    def remote(src, dst, to):
        i = used[0]
        used[0] += 1
        copy = pltpu.make_async_remote_copy(
            src_ref=src, dst_ref=dst, send_sem=send_sem.at[i], recv_sem=recv_sem.at[i],
            device_id=to, device_id_type=MESH,
        )
        sent.append(copy)
        copy.start()
        return copy

    n_local = [0]

    def local(src, dst):
        i = n_local[0]
        n_local[0] += 1
        copy = pltpu.make_async_copy(src, dst, loc_sem.at[i])
        copy.start()
        return copy

    xs_copy = local(frames.at[rec, pl.ds(c * OWN, OWN), :], xs.at[pl.ds(0, OWN)])
    own_copies = [
        local(wq, wq_b.at[0, 0]), local(wk, wk_b.at[0, 0]), local(wv, wv_b.at[0, 0]),
        local(wo, wo_b.at[0, 0]),
    ]
    for j in range(2):
        own_copies.append(local(up.at[:, pl.ds(j * 256, 256)], up_b.at[j, 0, 0]))

    def q_cols(step):
        return pl.ds(pl.multiple_of(((zl + step) % 4) * 256, 256), 256)

    for r in range(4):
        own_copies.append(local(dn.at[:, q_cols(r)], dn_b.at[r, 0, 0]))

    look_sem = n_local[0]
    n_local[0] += 1

    @pl.when(c == 0)
    def _():
        pltpu.make_async_copy(
            frames.at[rec, pl.ds(OWN, LOOK), :], xs.at[pl.ds(OWN, LOOK)], loc_sem.at[look_sem]
        ).start()

    barrier = pltpu.get_barrier_semaphore()

    def greet(i, carry):
        pl.semaphore_signal(barrier, inc=1, device_id=((tm + i) % 32, mp), device_id_type=MESH)
        return carry

    lax.fori_loop(1, 32, greet, 0)

    def greet_mp(i, carry):
        pl.semaphore_signal(barrier, inc=1, device_id=(tm, (mp + i) % 8), device_id_type=MESH)
        return carry

    lax.fori_loop(1, 8, greet_mp, 0)
    for step in (1, -1, 2, -2):
        pl.semaphore_signal(barrier, inc=1, device_id=z_dev(step), device_id_type=MESH)
    pl.semaphore_wait(barrier, 31 + 7 + 4)

    lx = (x + c) % 4
    ly = (y + c) % 4

    def at_x(label):
        return dev((label + 4 - c) % 4, y, z, c)

    def at_y(label):
        return dev(x, (label + 4 - c) % 4, z, c)

    def first(label):
        return label + 1 - 2 * (label % 2)

    def second(label):
        return 3 - label

    events = []

    class Half:
        def __init__(self, kind, source, view, base, rows):
            self.source, self.view, self.base, self.rows = source, view, base, rows
            if kind == 0:
                self.a, self.b, self.at_a, self.at_b = lx, ly, at_x, at_y
            else:
                self.a, self.b, self.at_a, self.at_b = ly, lx, at_y, at_x
            self.far = 2 if kind == 0 else -2

        def span(self, index, count):
            return pl.ds(pl.multiple_of(self.base + index * self.rows, self.rows), count * self.rows)

        def z(self):
            here = self.span(self.b * 4 + self.a, 1)
            self.arrive = [
                remote(self.source(1, here), self.view(0, pl.ds(3, 1), here), z_dev(1)),
                remote(self.source(-1, here), self.view(0, pl.ds(1, 1), here), z_dev(-1)),
                remote(self.source(self.far, here), self.view(0, pl.ds(2, 1), here), z_dev(self.far)),
            ]

        def hop(self, rows, to):
            for copy in self.arrive:
                copy.wait_recv()
            part = self.view(0, pl.ds(1, 3), rows)
            self.arrive = [remote(part, part, to)]

        def s1(self):
            self.hop(self.span(self.b * 4 + self.a, 1), self.at_a(first(self.a)))

        def s2(self):
            self.hop(self.span(self.b * 4 + 2 * (self.a // 2), 2), self.at_a(second(self.a)))

        def s3(self):
            self.hop(self.span(self.b * 4, 4), self.at_b(first(self.b)))

        def s4(self):
            near = self.span(8 * (self.b // 2), 8)
            self.hop(near, self.at_b(second(self.b)))
            self.share = [
                remote(self.view(0, pl.ds(1, 3), near), self.view(1, pl.ds(1, 3), near), sibling)
            ]

        def s5(self):
            for copy in self.arrive:
                copy.wait_recv()
            rest = self.span(8 - 8 * (self.b // 2), 8)
            self.share.append(
                remote(self.view(0, pl.ds(1, 3), rest), self.view(1, pl.ds(1, 3), rest), sibling)
            )

        def s6(self):
            for copy in self.share:
                copy.wait_recv()

    class Group:
        def __init__(self, halves, own, own_src):
            self.halves = halves
            self.own, self.own_src = own, own_src

        def z(self):
            for half in self.halves:
                half.z()
            self.own_copies = [
                remote(src, dst.at[pl.ds(1, 1), pl.ds(0, 1)], sibling)
                for src, dst in zip(self.own_src, self.own)
            ]

        def run(self, stage):
            if stage == 0:
                return self.z()
            for half in self.halves:
                getattr(half, "s%d" % stage)()
            if stage == 6:
                for copy in self.own_copies:
                    copy.wait_recv()

    def four(ref, rows, columns):
        return ref.reshape(1, 1, rows, columns)

    def half_kv(kind, ref, buf):
        return Half(
            kind,
            lambda step, rows: four(ref, D, 128).at[0, :, rows, :],
            lambda e, d, rows: buf.at[e, d, rows, :],
            0, 64,
        )

    def half_up(kind, j):
        return Half(
            kind,
            lambda step, rows: four(up, D, 512).at[0, :, rows, pl.ds(j * 256, 256)],
            lambda e, d, rows: up_b.at[j, e, d, rows, :],
            kind * 512, 32,
        )

    def half_dn(kind, r):
        return Half(
            kind,
            lambda step, rows: four(dn, 512, D).at[0, :, rows, q_cols(r + step + 4)],
            lambda e, d, rows: dn_b.at[r, e, d, rows, :],
            kind * 256, 16,
        )

    groups = {
        "kv": Group([half_kv(0, wk, wk_b), half_kv(1, wv, wv_b)], [wk_b, wv_b],
                    [four(wk, D, 128), four(wv, D, 128)]),
    }
    for j in range(2):
        groups["u%d" % j] = Group(
            [half_up(0, j), half_up(1, j)], [up_b.at[j]],
            [four(up, D, 512).at[:, :, :, pl.ds(j * 256, 256)]],
        )
    for r in range(4):
        groups["d%d" % r] = Group(
            [half_dn(0, r), half_dn(1, r)], [dn_b.at[r]],
            [four(dn, 512, D).at[:, :, :, q_cols(r)]],
        )

    class Ring:
        def __init__(self, ref, buf, rows):
            self.ref, self.buf, self.rows = ref, buf, rows

        def run(self, stage):
            buf, half = self.buf, self.rows // 2
            if stage == 0:
                self.up = remote(self.ref, buf.at[0, 3], z_dev(1))
                self.down = remote(self.ref, buf.at[0, 1], z_dev(-1))
                self.share = [remote(self.ref, buf.at[1, 0], sibling)]
            elif stage == 1:
                self.up.wait_recv()
                self.down.wait_recv()
                high, low = pl.ds(half, half), pl.ds(0, half)
                self.far = [
                    remote(buf.at[0, 3, high], buf.at[0, 2, high], z_dev(1)),
                    remote(buf.at[0, 1, low], buf.at[0, 2, low], z_dev(-1)),
                ]
                self.share.append(remote(buf.at[0, 1], buf.at[1, 1], sibling))
                self.share.append(remote(buf.at[0, 3], buf.at[1, 3], sibling))
            elif stage == 2:
                for copy in self.far:
                    copy.wait_recv()
                self.share.append(remote(buf.at[0, 2], buf.at[1, 2], sibling))
            else:
                for copy in self.share:
                    copy.wait_recv()

    groups["wq"] = Ring(wq, wq_b, D)
    groups["wo"] = Ring(wo, wo_b, 128)

    plan = {
        "wq": (0.1, 6.0, 9.0, 11.0),
        "kv": (0.0, 1.5, 3.0, 5.0, 8.0, 13.0, 15.0),
        "u0": (0.3, 3.2, 5.2, 9.0, 13.1, 18.0, 20.0),
        "wo": (6.1, 12.0, 15.1, 17.0),
        "u1": (4.0, 9.1, 11.0, 14.0, 18.1, 25.0, 27.0),
        "d2": (8.0, 14.1, 16.0, 18.2, 25.1, 29.0, 30.5),
        "d1": (12.0, 18.3, 20.0, 25.2, 29.1, 33.0, 34.5),
        "d3": (16.0, 22.0, 24.0, 29.2, 33.1, 37.0, 38.5),
        "d0": (20.0, 26.0, 28.0, 33.2, 37.1, 41.0, 42.5),
    }
    order = list(plan)
    for name in order:
        for stage, when in enumerate(plan[name]):
            events.append((when, order.index(name), name, stage))
    events.sort()

    def pump(until):
        while events and events[0][0] <= until:
            _, _, name, stage = events.pop(0)
            groups[name].run(stage)

    def need(name, stage):
        while any(e[2] == name and e[3] <= stage for e in events):
            _, _, other, step = events.pop(0)
            groups[other].run(step)

    pump(0.2)
    halo_i = used[0]
    used[0] += 1
    halo = pltpu.make_async_remote_copy(
        src_ref=frames.at[rec, pl.ds(0, LOOK), :], dst_ref=xs.at[pl.ds(OWN, LOOK)],
        send_sem=send_sem.at[halo_i], recv_sem=recv_sem.at[halo_i],
        device_id=((tm + 31) % 32, mp), device_id_type=MESH,
    )

    @pl.when(c == 1)
    def _():
        halo.start()

    pump(0.3)
    first_row = tm * 640 + c * OWN
    live_end = valid[rec] - first_row

    xs_copy.wait()

    def norm_rows(i, carry):
        rows = pl.ds(pl.multiple_of(i * 32, 32), 32)
        nrm[rows, :] = normalize(xs[rows, :].astype(F32), g1[...]).astype(BF16)
        return carry

    lax.fori_loop(0, 5, norm_rows, 0)
    pump(1.5)
    lax.fori_loop(5, 10, norm_rows, 0)
    pump(3.2)

    @pl.when(c == 0)
    def _():
        pltpu.make_async_copy(
            frames.at[rec, pl.ds(OWN, LOOK), :], xs.at[pl.ds(OWN, LOOK)], loc_sem.at[look_sem]
        ).wait()

    @pl.when(c == 1)
    def _():
        halo.wait()

    norm_rows(10, 0)
    row_i = lax.broadcasted_iota(jnp.int32, (16, OWN), 0)
    col_i = lax.broadcasted_iota(jnp.int32, (16, OWN), 1)
    inside = (col_i >= row_i * SEG) & (col_i < row_i * SEG + SEG) & (col_i < live_end)
    picks = jnp.where(inside, 1.0, 0.0)
    counts = jnp.sum(picks, -1, keepdims=True)
    nrm[ROWS:EXT, :] = (
        dot(picks.astype(BF16), nrm[:OWN, :]) / jnp.maximum(counts, 1.0)
    ).astype(BF16)
    pump(11.0)
    for copy in own_copies:
        copy.wait()

    def project(buf, dest, scale):
        def step(p, carry):
            e, d = p // 2, 2 * (p % 2)
            weight = jnp.concatenate([buf[e, d], buf[e, d + 1]], axis=1)
            value = dot(nrm[...], weight).astype(BF16) * scale
            dest[2 * p] = value[:, :128]
            dest[2 * p + 1] = value[:, 128:]
            return carry

        lax.fori_loop(0, 4, step, 0)

    need("wq", 3)
    project(wq_b, qb, jnp.asarray(0.125, BF16))
    need("kv", 6)
    project(wk_b, kb, jnp.asarray(1.0, BF16))
    project(wv_b, vb, jnp.asarray(1.0, BF16))
    pump(18.0)

    head_r = lax.broadcasted_iota(jnp.int32, (32, 128), 0) % 16
    head_l = lax.broadcasted_iota(jnp.int32, (32, 128), 1) // 64
    scores = jnp.zeros((32, ROWS), F32)
    for t in range(8):
        asked = qb[t, ROWS:EXT, :].astype(F32)
        rows = jnp.concatenate(
            [jnp.broadcast_to(asked[s : s + 1], (16, 128)) for s in range(2)], axis=0
        )
        rows = jnp.where(head_r == head_l + 2 * t, rows, 0.0).astype(BF16)
        scores = scores + dot_t(rows, kb[t, :ROWS, :])
    seg_r = lax.broadcasted_iota(jnp.int32, (32, ROWS), 0) // 16
    key_l = lax.broadcasted_iota(jnp.int32, (32, ROWS), 1)
    ok = (key_l >= seg_r * SEG) & (key_l < seg_r * SEG + KEYS) & (key_l < live_end)
    scores = jnp.where(ok, scores, NEG)
    p = jnp.exp(scores - jnp.max(scores, -1, keepdims=True))
    p = (p / jnp.sum(p, -1, keepdims=True)).astype(BF16)
    parts = []
    for t in range(8):
        got = dot(p, vb[t, :ROWS, :])
        got = jnp.where(head_r == head_l + 2 * t, got, 0.0)
        parts.append(
            jnp.concatenate(
                [jnp.sum(got[s * 16 : s * 16 + 16], 0, keepdims=True) for s in range(2)], axis=0
            )
        )
    summed = jnp.concatenate(parts, axis=1)
    summed = jnp.concatenate([summed, jnp.zeros((14, D), F32)], axis=0).astype(BF16)
    need("wo", 3)
    memory = dot(summed, wo_b[...].reshape(D, D)).astype(BF16).astype(F32)
    for s in range(2):
        for b in range(8):
            mrow[s * 8 + b : s * 8 + b + 1, :] = memory[s : s + 1, b * 128 : b * 128 + 128]
    mine = pl.ds(pl.multiple_of(c * 16, 16), 16)
    mem_b[tm, mine, :] = mrow[...].astype(BF16)
    pair = remote(mem_b.at[tm, mine], mem_b.at[tm, mine], sibling)
    pump(20.0)
    pair.wait_recv()

    base = used[0]
    used[0] += 31

    def bank_copy(i):
        return pltpu.make_async_remote_copy(
            src_ref=mem_b.at[tm], dst_ref=mem_b.at[tm],
            send_sem=send_sem.at[base + i], recv_sem=recv_sem.at[base + i],
            device_id=((tm + 1 + i) % 32, mp), device_id_type=MESH,
        )

    def bank_send(i, carry):
        bank_copy(i).start()
        return carry

    lax.fori_loop(0, 31, bank_send, 0)
    pump(25.2)

    def bank_wait(i, carry):
        bank_copy(i).wait()
        return carry

    lax.fori_loop(0, 31, bank_wait, 0)

    memf[...] = mem_b[...].reshape(SLOTS * 8, 128).astype(F32)
    mem = jnp.concatenate(
        [memf[pl.ds(b, SLOTS, stride=8), :] for b in range(8)], axis=1
    ).astype(BF16)

    def bank_project(buf, dest):
        def step(p, carry):
            e, d = p // 2, 2 * (p % 2)
            weight = jnp.concatenate([buf[e, d], buf[e, d + 1]], axis=1)
            value = dot(mem, weight).astype(BF16)
            dest[2 * p] = value[:, :128]
            dest[2 * p + 1] = value[:, 128:]
            return carry

        lax.fori_loop(0, 4, step, 0)

    bank_project(wk_b, bk)
    bank_project(wv_b, bv)
    pump(28.0)

    lane = lax.broadcasted_iota(jnp.int32, (SEG, 128), 1)
    near_l = lax.broadcasted_iota(jnp.int32, (2 * SEG, KEYS), 1)
    far_l = lax.broadcasted_iota(jnp.int32, (2 * SEG, SLOTS), 1)
    for s in range(2):
        near_ok = near_l < live_end - s * SEG
        far_ok = (far_l < tm * 4 + c * 2 + s) & (far_l * SEG < live_end + first_row)
        rows, keys = slice(s * SEG, s * SEG + SEG), slice(s * SEG, s * SEG + KEYS)

        def heads(t, carry, rows=rows, keys=keys, near_ok=near_ok, far_ok=far_ok):
            q = qb[t, rows, :]
            zero = jnp.zeros_like(q)
            q = jnp.concatenate([jnp.where(lane < 64, q, zero), jnp.where(lane < 64, zero, q)], 0)
            near = jnp.where(near_ok, dot_t(q, kb[t, keys, :]), NEG)
            far = jnp.where(far_ok, dot_t(q, bk[t]), NEG)
            top = jnp.maximum(jnp.max(near, -1, keepdims=True), jnp.max(far, -1, keepdims=True))
            near = jnp.exp(near - top)
            far = jnp.exp(far - top)
            total = jnp.sum(near, -1, keepdims=True) + jnp.sum(far, -1, keepdims=True)
            got = dot(near.astype(BF16), vb[t, keys, :]) + dot(far.astype(BF16), bv[t])
            got = got / total
            got = jnp.where(lane < 64, got[:SEG], got[SEG:]).astype(BF16)
            fo[rows, pl.ds(pl.multiple_of(t * 128, 128), 128)] = got
            return carry

        lax.fori_loop(0, 4, heads, 0)
        pump(29.0 + 4 * s)
        lax.fori_loop(4, 8, heads, 0)
        pump(30.5 + 4 * s)

    for n in range(4):
        weight = wo_b[:, :, :, n * 256 : n * 256 + 256].reshape(D, 256)
        mixed[n] = dot(fo[...], weight) + xs[:OWN, n * 256 : n * 256 + 256].astype(F32)
    pump(36.0)

    def norm_two(i, carry):
        rows = pl.ds(pl.multiple_of(i * 32, 32), 32)
        v = jnp.concatenate([mixed[n, rows, :] for n in range(4)], axis=1)
        n2[rows, :] = normalize(v, g2[...]).astype(BF16)
        return carry

    lax.fori_loop(0, 10, norm_two, 0)

    for j in range(2):
        need("u%d" % j, 6)

        def up_step(b, carry, j=j):
            h = dot(n2[...], up_b[j, b // 4, b % 4])
            h = 0.5 * h * (1.0 + lax.erf(h * (2.0 ** -0.5)))
            hid[:, pl.ds(pl.multiple_of(b * 512 + j * 256, 256), 256)] = h.astype(BF16)
            return carry

        for k in range(4):
            lax.fori_loop(2 * k, 2 * k + 2, up_step, 0)
            pump(36.0 + 4 * j + k)

    outs = []
    row_span = pl.ds(pl.multiple_of(c * OWN, OWN), OWN)
    for r in (2, 1, 3, 0):
        need("d%d" % r, 6)
        block = dot(hid[...], dn_b[r].reshape(4 * D, 256))
        to = (zl + r) % 4
        block = (block + mixed[to]).astype(BF16)
        ob[r, 0] = block[:, :128]
        ob[r, 1] = block[:, 128:]
        if r:
            for e in range(2):
                core = c if e == 0 else 1 - c
                outs.append(remote(ob.at[r, core], out.at[rec, row_span, :], (tm, to * 2 + core)))
        else:
            outs.append(remote(ob.at[0, 1 - c], out.at[rec, row_span, :], sibling))
            home = local(ob.at[0, c], out.at[rec, row_span, :])
    home.wait()
    for copy in outs:
        copy.wait_recv()
    for copy in sent:
        copy.wait_send()
    assert used[0] <= N_SEM, used[0]


def body(frames, valid, ln1_gain, w_query, w_key, w_value, w_out, ln2_gain, w_up, w_down):
    vmem = pl.BlockSpec(memory_space=pltpu.VMEM)
    anywhere = pl.BlockSpec(memory_space=pl.ANY)
    scratch = [
        pltpu.VMEM((ROWS, D), BF16),
        pltpu.VMEM((EXT, D), BF16),
        pltpu.VMEM((8, EXT, 128), BF16),
        pltpu.VMEM((8, EXT, 128), BF16),
        pltpu.VMEM((8, EXT, 128), BF16),
        pltpu.VMEM((2, 4, D, 128), BF16),
        pltpu.VMEM((2, 4, D, 128), BF16),
        pltpu.VMEM((2, 4, D, 128), BF16),
        pltpu.VMEM((2, 4, 128, D), BF16),
        pltpu.VMEM((2, 2, 4, D, 256), BF16),
        pltpu.VMEM((4, 2, 4, 512, 256), BF16),
        pltpu.VMEM((16, 128), F32),
        pltpu.VMEM((32, 32, 128), BF16),
        pltpu.VMEM((SLOTS * 8, 128), F32),
        pltpu.VMEM((8, SLOTS, 128), BF16),
        pltpu.VMEM((8, SLOTS, 128), BF16),
        pltpu.VMEM((OWN, D), BF16),
        pltpu.VMEM((4, OWN, 256), F32),
        pltpu.VMEM((OWN, D), BF16),
        pltpu.VMEM((OWN, 4 * D), BF16),
        pltpu.VMEM((4, 2, OWN, 128), BF16),
        pltpu.SemaphoreType.DMA((16,)),
        pltpu.SemaphoreType.DMA((N_SEM,)),
        pltpu.SemaphoreType.DMA((N_SEM,)),
    ]
    return pl.pallas_call(
        kernel,
        name="layer",
        out_shape=jax.ShapeDtypeStruct((frames.shape[0], frames.shape[1], 128), BF16),
        in_specs=[pl.BlockSpec(memory_space=pltpu.SMEM), vmem, vmem] + [anywhere] * 7,
        out_specs=anywhere,
        scratch_shapes=scratch,
        compiler_params=pltpu.CompilerParams(
            collective_id=0, has_side_effects=True, vmem_limit_bytes=56 * 2**20
        ),
    )(
        valid, ln1_gain.reshape(1, D), ln2_gain.reshape(1, D),
        frames, w_query, w_key, w_value, w_out, w_up, w_down,
    )


def solution(mesh):
    placed = (
        P(None, "tm", None),
        P(),
        P(),
        P(None, "mp"),
        P(None, "mp"),
        P(None, "mp"),
        P("mp", None),
        P(),
        P(None, "mp"),
        P("mp", None),
    )
    return jax.shard_map(
        body, mesh=mesh, in_specs=placed, out_specs=P(None, "tm", "mp"), check_vma=False
    )
```

profile of v0, /device:TPU:1, one launch (start us, length us, event | category | flops | bytes accessed | tf_op | source)
XLA Modules:
  0.0 123.6 jit_solution(14214372583530705693)
XLA Ops:
  0.0 121.6 %layer.1 = bf16[4,640,128]{2,1,0:T(8,128)(2,1)} custom-call(s32[4]{0:T(128)} %valid.1, f32[1,1024]{1,0:T(1,128)} %bitcast.2, f32[1,1024]{1,0:T(1,128)} %bitcast.3, bf16[4,640,1024]{2,1,0:T(8,128)(2,1)} %frames.1, bf16[1024,128]{1,0:T(8,128)(2,1)} %wq.1, bf16[1024,128]{1,0:T(8,128)(2,1)} %wk.1, bf16[1024,128]{1,0:T(8,128)(2,1)} %wv.1, bf16[128,1024]{1,0:T(8,128)(2,1)} %wo.1, ...), custom_call_target="tpu_custom_call" | custom-call | tf_op jit(solution)/shard_map/layer/pallas_call | solution.py:577
  121.6 2.0 %copy.12 = bf16[4,640,128]{2,1,0:T(8,128)(2,1)} copy(bf16[4,640,128]{2,1,0:T(8,128)(2,1)} %layer.1) | data formatting | bytes 1310720
where the time goes:
time: 124 us
  Pallas kernels  122 us (98%)
  local copies, waits for them, and re-layouts  1.97 us (2%)
    pallas_call x1, Pallas kernels, body(): pl.pallas_call(kernel, name='layer', out_shape=jax.ShapeDtypeStruct((fram...  122 us

commit v1 on v0

v1 whole, which is shorter than its diff:
```python
import jax
import jax.numpy as jnp
from jax import lax
from jax.experimental import pallas as pl
from jax.experimental.pallas import tpu as pltpu
from jax.sharding import PartitionSpec as P

MESH = pl.DeviceIdType.MESH
F32 = jnp.float32
BF16 = jnp.bfloat16

D = 1024
SEG = 160
LOOK = 32
KEYS = SEG + LOOK
OWN = 2 * SEG
ROWS = OWN + LOOK
EXT = ROWS + 16
SLOTS = 128
EPS = 1e-05
NEG = -1e30
N_SEM = 232

SCHEDULE = (
    "norm_one enter k:0 v:0",
    "wq:0 look k:1 v:1",
    "u0:0 k:2 meet sums",
    "v:2 wq:1 wo:0 k:3",
    "u1:0 v:3 u0:1 d2:0",
    "wq:2 k:4 k0 v:4",
    "d1:0 k:5 k1 d3:0",
    "wo:1 u0:2 v0 v:5",
    "v1 d0:0 u1:1 d2:1",
    "d1:1 d3:1 wo:2 q0",
    "u0:3 wq:3 q1 summary",
    "u1:2 d0:1 wo:3 memory",
    "d2:2 near0 d1:2 bank_a",
    "d3:2 near1 near2 near3",
    "u0:4 u1:3 bank_b d0:2",
    "d2:3 d1:3 d3:3 bank_c",
    "bank_d far0 u1:4 far1",
    "far2 d0:3 far3 d2:4",
    "mix norm_two d1:4 up00",
    "up01 u0:5 up02 d3:4",
    "up03 up10 d0:4 up11",
    "u1:5 up12 up13 d2:5",
    "down2 d1:5 down1 d3:5",
    "down3 d0:5 down0",
)


def dot(a, b):
    return jnp.dot(a, b, preferred_element_type=F32)


def normalize(x, gain):
    mean = jnp.sum(x, -1, keepdims=True) * (1.0 / D)
    square = jnp.sum(x * x, -1, keepdims=True) * (1.0 / D)
    return (x - mean) * lax.rsqrt(square - mean * mean + EPS) * gain


def kernel(
    valid, g1, g2, frames, wq, wk, wv, wo, up, dn, out,
    xs, nrm, qb, kt, vb, wq_b, wk_b, wv_b, wo_b, up_b, dn_b,
    mrow, mem_b, memf, bk, bv, acc, mx, fo, mixed, n2, hid, ob,
    loc_sem, send_sem, recv_sem, hello,
):
    tm = lax.axis_index("tm")
    mp = lax.axis_index("mp")
    x = tm // 8
    y = (tm // 2) % 4
    zl = mp // 2
    z = (tm % 2) * 4 + zl
    c = mp % 2
    rec = zl

    def dev(px, py, pz, pc):
        return ((px * 4 + py) * 2 + pz // 4, (pz % 4) * 2 + pc)

    def z_dev(step):
        return dev(x, y, (z + step + 8) % 8, c)

    sibling = (tm, zl * 2 + 1 - c)

    barrier = pltpu.get_barrier_semaphore()

    across = ((zl + 2) % 4) * 2 + c
    before, after = ((tm + 31) % 32, across), ((tm + 1) % 32, across)
    greeted = [before, after] + [z_dev(step) for step in (1, -1, 2, -2)]
    greeted += [(tm, (mp + i) % 8) for i in range(1, 8)]
    along = [dev((x + i) % 4, y, z, c) for i in (2, 1, 3)]
    bank_one = [dev((x + i) % 4, y, (z + 4) % 8, c) for i in (2, 1, 3, 0)] + along
    bank_two = [dev(x, (y + i) % 4, z, c) for i in (2, 1, 3)]
    greeted += along + bank_two
    for other in greeted:
        pl.semaphore_signal(barrier, inc=1, device_id=other, device_id_type=MESH)

    used = [0]
    sent = []

    def remote(src, dst, to):
        i = used[0]
        used[0] += 1
        copy = pltpu.make_async_remote_copy(
            src_ref=src, dst_ref=dst, send_sem=send_sem.at[i], recv_sem=recv_sem.at[i],
            device_id=to, device_id_type=MESH,
        )
        sent.append(copy)
        copy.start()
        return copy

    n_local = [0]

    def local(src, dst):
        i = n_local[0]
        n_local[0] += 1
        copy = pltpu.make_async_copy(src, dst, loc_sem.at[i])
        copy.start()
        return copy

    xs_copy = local(frames.at[rec, pl.ds(c * OWN, OWN), :], xs.at[pl.ds(0, OWN)])
    own_copies = [
        local(wq, wq_b.at[0, 0]), local(wk, wk_b.at[0, 0]), local(wv, wv_b.at[0, 0]),
        local(wo, wo_b.at[0, 0]),
    ]
    for j in range(2):
        own_copies.append(local(up.at[:, pl.ds(j * 256, 256)], up_b.at[j, 0, 0]))

    def q_cols(step):
        return pl.ds(pl.multiple_of(((zl + step) % 4) * 256, 256), 256)

    for r in range(4):
        own_copies.append(local(dn.at[:, q_cols(r)], dn_b.at[r, 0, 0]))

    look_sem = n_local[0]
    n_local[0] += 1

    @pl.when(c == 0)
    def _():
        pltpu.make_async_copy(
            frames.at[rec, pl.ds(OWN, LOOK), :], xs.at[pl.ds(OWN, LOOK)], loc_sem.at[look_sem]
        ).start()

    lx = (x + c) % 4
    ly = (y + c) % 4

    def at_x(label):
        return dev((label + 4 - c) % 4, y, z, c)

    def at_y(label):
        return dev(x, (label + 4 - c) % 4, z, c)

    def first(label):
        return label + 1 - 2 * (label % 2)

    def second(label):
        return 3 - label

    class Half:
        def __init__(self, kind, source, view, base, rows):
            self.source, self.view, self.base, self.rows = source, view, base, rows
            if kind == 0:
                self.a, self.b, self.at_a, self.at_b = lx, ly, at_x, at_y
            else:
                self.a, self.b, self.at_a, self.at_b = ly, lx, at_y, at_x
            self.far = 2 if kind == 0 else -2

        def span(self, index, count):
            return pl.ds(pl.multiple_of(self.base + index * self.rows, self.rows), count * self.rows)

        def z(self):
            here = self.span(self.b * 4 + self.a, 1)
            self.arrive = [
                remote(self.source(1, here), self.view(0, pl.ds(3, 1), here), z_dev(1)),
                remote(self.source(-1, here), self.view(0, pl.ds(1, 1), here), z_dev(-1)),
                remote(self.source(self.far, here), self.view(0, pl.ds(2, 1), here), z_dev(self.far)),
            ]

        def hop(self, rows, to):
            for copy in self.arrive:
                copy.wait_recv()
            part = self.view(0, pl.ds(1, 3), rows)
            self.arrive = [remote(part, part, to)]

        def s1(self):
            for copy in self.arrive:
                copy.wait_recv()
            part = self.view(0, pl.ds(1, 3), self.span(self.b * 4 + self.a, 1))
            self.arrive = [remote(part, part, self.at_a((self.a + i) % 4)) for i in (2, 1, 3)]

        def s2(self):
            self.hop(self.span(self.b * 4, 4), self.at_b(first(self.b)))

        def s3(self):
            near = self.span(8 * (self.b // 2), 8)
            self.hop(near, self.at_b(second(self.b)))
            self.share = [
                remote(self.view(0, pl.ds(1, 3), near), self.view(1, pl.ds(1, 3), near), sibling)
            ]

        def s4(self):
            for copy in self.arrive:
                copy.wait_recv()
            rest = self.span(8 - 8 * (self.b // 2), 8)
            self.share.append(
                remote(self.view(0, pl.ds(1, 3), rest), self.view(1, pl.ds(1, 3), rest), sibling)
            )

        def s5(self):
            for copy in self.share:
                copy.wait_recv()

    class Group:
        def __init__(self, halves, own, own_src):
            self.halves = halves
            self.own, self.own_src = own, own_src

        def z(self):
            for half in self.halves:
                half.z()
            self.own_copies = [
                remote(src, dst.at[pl.ds(1, 1), pl.ds(0, 1)], sibling)
                for src, dst in zip(self.own_src, self.own)
            ]

        def run(self, stage):
            if stage == 0:
                return self.z()
            for half in self.halves:
                getattr(half, "s%d" % stage)()
            if stage == 5:
                for copy in self.own_copies:
                    copy.wait_recv()

    def four(ref, rows, columns):
        return ref.reshape(1, 1, rows, columns)

    def half_kv(kind, ref, buf):
        return Half(
            kind,
            lambda step, rows: four(ref, D, 128).at[0, :, rows, :],
            lambda e, d, rows: buf.at[e, d, rows, :],
            kind * 512, 32,
        )

    def half_up(kind, j):
        return Half(
            kind,
            lambda step, rows: four(up, D, 512).at[0, :, rows, pl.ds(j * 256, 256)],
            lambda e, d, rows: up_b.at[j, e, d, rows, :],
            kind * 512, 32,
        )

    def half_dn(kind, r):
        return Half(
            kind,
            lambda step, rows: four(dn, 512, D).at[0, :, rows, q_cols(r + step + 4)],
            lambda e, d, rows: dn_b.at[r, e, d, rows, :],
            kind * 256, 16,
        )

    groups = {
        "k": Group([half_kv(0, wk, wk_b), half_kv(1, wk, wk_b)], [wk_b], [four(wk, D, 128)]),
        "v": Group([half_kv(0, wv, wv_b), half_kv(1, wv, wv_b)], [wv_b], [four(wv, D, 128)]),
    }
    for j in range(2):
        groups["u%d" % j] = Group(
            [half_up(0, j), half_up(1, j)], [up_b.at[j]],
            [four(up, D, 512).at[:, :, :, pl.ds(j * 256, 256)]],
        )
    for r in range(4):
        groups["d%d" % r] = Group(
            [half_dn(0, r), half_dn(1, r)], [dn_b.at[r]],
            [four(dn, 512, D).at[:, :, :, q_cols(r)]],
        )

    class Ring:
        def __init__(self, ref, buf, rows):
            self.ref, self.buf, self.rows = ref, buf, rows

        def run(self, stage):
            buf, half = self.buf, self.rows // 2
            if stage == 0:
                self.up = remote(self.ref, buf.at[0, 3], z_dev(1))
                self.down = remote(self.ref, buf.at[0, 1], z_dev(-1))
                self.share = [remote(self.ref, buf.at[1, 0], sibling)]
            elif stage == 1:
                self.up.wait_recv()
                self.down.wait_recv()
                high, low = pl.ds(half, half), pl.ds(0, half)
                self.far = [
                    remote(buf.at[0, 3, high], buf.at[0, 2, high], z_dev(1)),
                    remote(buf.at[0, 1, low], buf.at[0, 2, low], z_dev(-1)),
                ]
                self.share.append(remote(buf.at[0, 1], buf.at[1, 1], sibling))
                self.share.append(remote(buf.at[0, 3], buf.at[1, 3], sibling))
            elif stage == 2:
                for copy in self.far:
                    copy.wait_recv()
                self.share.append(remote(buf.at[0, 2], buf.at[1, 2], sibling))
            else:
                for copy in self.share:
                    copy.wait_recv()

    groups["wq"] = Ring(wq, wq_b, D)
    groups["wo"] = Ring(wo, wo_b, 128)

    halo_i = used[0]
    used[0] += 1
    halo = pltpu.make_async_remote_copy(
        src_ref=frames.at[(zl + 2) % 4, pl.ds(0, LOOK), :], dst_ref=xs.at[pl.ds(OWN, LOOK)],
        send_sem=send_sem.at[halo_i], recv_sem=recv_sem.at[halo_i],
        device_id=before, device_id_type=MESH,
    )
    first_row = tm * 640 + c * OWN
    live_end = valid[rec] - first_row
    acts = {}

    def action(f):
        acts[f.__name__] = f
        return f

    def loop(f, lo, hi, unroll=1):
        lax.fori_loop(lo, hi, lambda i, carry: (f(i), carry)[1], 0, unroll=unroll)

    @action
    def enter():
        pl.semaphore_wait(barrier, len(greeted))

    @action
    def look():
        pl.semaphore_signal(hello.at[0], inc=1, device_id=z_dev(-2), device_id_type=MESH)

        @pl.when(c == 1)
        def _():
            halo.start()

    @action
    def meet():
        pl.semaphore_wait(hello.at[0], 1)
        for other in along:
            pl.semaphore_signal(hello.at[1], inc=1, device_id=other, device_id_type=MESH)

    def norm_rows(i):
        rows = pl.ds(pl.multiple_of(i * 32, 32), 32)
        nrm[rows, :] = normalize(xs[rows, :].astype(F32), g1[...]).astype(BF16)

    @action
    def norm_one():
        xs_copy.wait()
        loop(norm_rows, 0, 10, unroll=2)

    @action
    def sums():
        @pl.when(c == 0)
        def _():
            pltpu.make_async_copy(
                frames.at[rec, pl.ds(OWN, LOOK), :], xs.at[pl.ds(OWN, LOOK)], loc_sem.at[look_sem]
            ).wait()

        @pl.when(c == 1)
        def _():
            halo.wait()

        norm_rows(10)
        row_i = lax.broadcasted_iota(jnp.int32, (16, OWN), 0)
        col_i = lax.broadcasted_iota(jnp.int32, (16, OWN), 1)
        inside = (col_i >= row_i * SEG) & (col_i < row_i * SEG + SEG) & (col_i < live_end)
        picks = jnp.where(inside, 1.0, 0.0)
        counts = jnp.sum(picks, -1, keepdims=True)
        nrm[ROWS:EXT, :] = (
            dot(picks.astype(BF16), nrm[:OWN, :]) / jnp.maximum(counts, 1.0)
        ).astype(BF16)
        for copy in own_copies:
            copy.wait()

    def project(left, buf, dest, p, scale=None):
        e, d = p // 2, 2 * (p % 2)
        weight = jnp.concatenate([buf[e, d], buf[e, d + 1]], axis=1)
        value = dot(left, weight).astype(BF16)
        if scale is not None:
            value = value * jnp.asarray(scale, BF16)
        dest[2 * p] = value[:, :128]
        dest[2 * p + 1] = value[:, 128:]

    def project_keys(p):
        e, d = p // 2, 2 * (p % 2)
        weight = jnp.concatenate([wk_b[e, d], wk_b[e, d + 1]], axis=1)
        value = dot(nrm[:ROWS, :], weight)
        for s in range(2):
            turned = value[s * SEG : s * SEG + KEYS].T.astype(BF16)
            kt[s, 2 * p] = turned[:128]
            kt[s, 2 * p + 1] = turned[128:]

    for e in range(2):
        span = (2 * e, 2 * e + 2)
        acts["q%d" % e] = lambda span=span: loop(
            lambda p: project(nrm[...], wq_b, qb, p, 0.125), *span)
        acts["k%d" % e] = lambda span=span: loop(project_keys, *span)
        acts["v%d" % e] = lambda span=span: loop(lambda p: project(nrm[...], wv_b, vb, p), *span)

    held = {}

    @action
    def summary():
        head_r = lax.broadcasted_iota(jnp.int32, (16, 128), 0)
        head_l = lax.broadcasted_iota(jnp.int32, (16, 128), 1) // 64
        key_l = lax.broadcasted_iota(jnp.int32, (16, KEYS), 1)
        parts = []
        for s in range(2):
            parts.append(jnp.zeros((16, KEYS), F32))
            for t in range(8):
                asked = qb[t, ROWS:EXT, :].astype(F32)
                rows = jnp.broadcast_to(asked[s : s + 1], (16, 128))
                rows = jnp.where(head_r == head_l + 2 * t, rows, 0.0).astype(BF16)
                parts[s] = parts[s] + dot(rows, kt[s, t])
            parts[s] = jnp.where(key_l < live_end - s * SEG, parts[s], NEG)
        scores = jnp.concatenate(parts, axis=0)
        p = jnp.exp(scores - jnp.max(scores, -1, keepdims=True))
        p = (p / jnp.sum(p, -1, keepdims=True)).astype(BF16)
        parts = []
        for t in range(8):
            rows = []
            for s in range(2):
                got = dot(p[s * 16 : s * 16 + 16], vb[t, s * SEG : s * SEG + KEYS, :])
                got = jnp.where(head_r == head_l + 2 * t, got, 0.0)
                rows.append(jnp.sum(got, 0, keepdims=True))
            parts.append(jnp.concatenate(rows, axis=0))
        summed = jnp.concatenate(parts, axis=1)
        held["summed"] = jnp.concatenate([summed, jnp.zeros((14, D), F32)], axis=0).astype(BF16)

    mine = pl.ds(pl.multiple_of(c * 16, 16), 16)
    zh = tm % 2

    @action
    def memory():
        got = dot(held["summed"], wo_b[...].reshape(D, D)).astype(BF16).astype(F32)
        for s in range(2):
            for b in range(8):
                mrow[s * 8 + b : s * 8 + b + 1, :] = got[s : s + 1, b * 128 : b * 128 + 128]
        mem_b[x, y, zh, mine, :] = mrow[...].astype(BF16)
        part = mem_b.at[x, y, zh, mine]
        held["pair"] = remote(part, part, sibling)

    @action
    def bank_a():
        pl.semaphore_wait(hello.at[1], 3)
        held["pair"].wait_recv()
        part = mem_b.at[x, y, zh]
        held["bank"] = [remote(part, part, other) for other in bank_one]

    @action
    def bank_b():
        for copy in held["bank"]:
            copy.wait_recv()
        part = mem_b.at[:, pl.ds(y, 1)]
        held["bank"] = [remote(part, part, other) for other in bank_two]

    @action
    def bank_c():
        for copy in held["bank"]:
            copy.wait_recv()
        memf[...] = mem_b[...].reshape(SLOTS * 8, 128).astype(F32)
        mem = jnp.concatenate(
            [memf[pl.ds(b, SLOTS, stride=8), :] for b in range(8)], axis=1
        ).astype(BF16)
        held["mem"] = mem

        def keys(p):
            e, d = p // 2, 2 * (p % 2)
            weight = jnp.concatenate([wk_b[e, d], wk_b[e, d + 1]], axis=1)
            turned = dot(mem, weight).T.astype(BF16)
            bk[2 * p] = turned[:128]
            bk[2 * p + 1] = turned[128:]

        loop(keys, 0, 4)

    @action
    def bank_d():
        mem = held["mem"]
        loop(lambda p: project(mem, wv_b, bv, p), 0, 4)

    lane = lax.broadcasted_iota(jnp.int32, (SEG, 128), 1)

    def one_head(s, t, h):
        q = qb[t, s * SEG : s * SEG + SEG, :]
        mine = lane < 64 if h == 0 else lane >= 64
        return jnp.where(mine, q, jnp.zeros_like(q))

    def with_ones(v):
        return jnp.concatenate([v, jnp.ones_like(v)], axis=1)

    def near_step(s, t):
        keys = slice(s * SEG, s * SEG + KEYS)
        near_l = lax.broadcasted_iota(jnp.int32, (SEG, KEYS), 1)
        ones = with_ones(vb[t, keys, :])
        for h in range(2):
            near = dot(one_head(s, t, h), kt[s, t])
            near = jnp.where(near_l < live_end - s * SEG, near, NEG)
            top = jnp.max(near, -1, keepdims=True)
            near = jnp.exp(near - top).astype(BF16)
            rows = slice(h * SEG, h * SEG + SEG)
            acc[s * 8 + t, rows] = dot(near, ones)
            mx[s * 8 + t, rows] = jnp.broadcast_to(top, (SEG, 128))

    def far_step(s, t):
        far_l = lax.broadcasted_iota(jnp.int32, (SEG, SLOTS), 1)
        far_ok = (far_l < tm * 4 + c * 2 + s) & (far_l * SEG < live_end + first_row)
        both = []
        for h in range(2):
            rows = slice(h * SEG, h * SEG + SEG)
            far = jnp.where(far_ok, dot(one_head(s, t, h), bk[t]), NEG)
            before = mx[s * 8 + t, rows]
            top = jnp.maximum(before, jnp.max(far, -1, keepdims=True))
            far = jnp.exp(far - top).astype(BF16)
            keep = jnp.exp(before - top)
            got = dot(far, with_ones(bv[t]))
            total = acc[s * 8 + t, rows, 128:] * keep + got[:, 128:]
            both.append((acc[s * 8 + t, rows, :128] * keep + got[:, :128]) / total)
        got = jnp.where(lane < 64, both[0], both[1]).astype(BF16)
        fo[s * SEG : s * SEG + SEG, pl.ds(pl.multiple_of(t * 128, 128), 128)] = got

    for s in range(2):
        for half in range(2):
            span = (4 * half, 4 * half + 4)
            acts["near%d" % (2 * s + half)] = lambda s=s, span=span: loop(
                lambda t: near_step(s, t), *span, unroll=2)
            acts["far%d" % (2 * s + half)] = lambda s=s, span=span: loop(
                lambda t: far_step(s, t), *span, unroll=2)

    @action
    def mix():
        for n in range(4):
            weight = wo_b[:, :, :, n * 256 : n * 256 + 256].reshape(D, 256)
            mixed[n] = dot(fo[...], weight) + xs[:OWN, n * 256 : n * 256 + 256].astype(F32)

    @action
    def norm_two():
        def step(i):
            rows = pl.ds(pl.multiple_of(i * 32, 32), 32)
            v = jnp.concatenate([mixed[n, rows, :] for n in range(4)], axis=1)
            n2[rows, :] = normalize(v, g2[...]).astype(BF16)

        loop(step, 0, 10, unroll=2)

    def up_step(j, b):
        h = dot(n2[...], up_b[j, b // 4, b % 4])
        h = 0.5 * h * (1.0 + lax.erf(h * (2.0 ** -0.5)))
        hid[:, pl.ds(pl.multiple_of(b * 512 + j * 256, 256), 256)] = h.astype(BF16)

    for j in range(2):
        for k in range(4):
            acts["up%d%d" % (j, k)] = lambda j=j, k=k: loop(
                lambda b: up_step(j, b), 2 * k, 2 * k + 2)

    outs = []
    row_span = pl.ds(pl.multiple_of(c * OWN, OWN), OWN)

    def down(r):
        block = dot(hid[...], dn_b[r].reshape(4 * D, 256))
        to = (zl + r) % 4
        block = (block + mixed[to]).astype(BF16)
        ob[r, 0] = block[:, :128]
        ob[r, 1] = block[:, 128:]
        if r:
            for core in (c, 1 - c):
                outs.append(remote(ob.at[r, core], out.at[rec, row_span, :], (tm, to * 2 + core)))
        else:
            outs.append(remote(ob.at[0, 1 - c], out.at[rec, row_span, :], sibling))
            held["home"] = local(ob.at[0, c], out.at[rec, row_span, :])

    for r in range(4):
        acts["down%d" % r] = lambda r=r: down(r)

    for token in " ".join(SCHEDULE).split():
        if ":" in token:
            name, stage = token.split(":")
            groups[name].run(int(stage))
        else:
            acts[token]()
    held["home"].wait()
    for copy in outs:
        copy.wait_recv()
    for copy in sent:
        copy.wait_send()
    assert used[0] <= N_SEM, used[0]


def body(frames, valid, ln1_gain, w_query, w_key, w_value, w_out, ln2_gain, w_up, w_down):
    vmem = pl.BlockSpec(memory_space=pltpu.VMEM)
    anywhere = pl.BlockSpec(memory_space=pl.ANY)
    scratch = [
        pltpu.VMEM((ROWS, D), BF16),
        pltpu.VMEM((EXT, D), BF16),
        pltpu.VMEM((8, EXT, 128), BF16),
        pltpu.VMEM((2, 8, 128, KEYS), BF16),
        pltpu.VMEM((8, EXT, 128), BF16),
        pltpu.VMEM((2, 4, D, 128), BF16),
        pltpu.VMEM((2, 4, D, 128), BF16),
        pltpu.VMEM((2, 4, D, 128), BF16),
        pltpu.VMEM((2, 4, 128, D), BF16),
        pltpu.VMEM((2, 2, 4, D, 256), BF16),
        pltpu.VMEM((4, 2, 4, 512, 256), BF16),
        pltpu.VMEM((16, 128), F32),
        pltpu.VMEM((4, 4, 2, 32, 128), BF16),
        pltpu.VMEM((SLOTS * 8, 128), F32),
        pltpu.VMEM((8, SLOTS, 128), BF16),
        pltpu.VMEM((8, SLOTS, 128), BF16),
        pltpu.VMEM((16, OWN, 256), F32),
        pltpu.VMEM((16, OWN, 128), F32),
        pltpu.VMEM((OWN, D), BF16),
        pltpu.VMEM((4, OWN, 256), F32),
        pltpu.VMEM((OWN, D), BF16),
        pltpu.VMEM((OWN, 4 * D), BF16),
        pltpu.VMEM((4, 2, OWN, 128), BF16),
        pltpu.SemaphoreType.DMA((16,)),
        pltpu.SemaphoreType.DMA((N_SEM,)),
        pltpu.SemaphoreType.DMA((N_SEM,)),
        pltpu.SemaphoreType.REGULAR((2,)),
    ]
    return pl.pallas_call(
        kernel,
        name="layer",
        out_shape=jax.ShapeDtypeStruct((frames.shape[0], frames.shape[1], 128), BF16),
        in_specs=[pl.BlockSpec(memory_space=pltpu.SMEM), vmem, vmem] + [anywhere] * 7,
        out_specs=anywhere,
        scratch_shapes=scratch,
        compiler_params=pltpu.CompilerParams(
            collective_id=0, has_side_effects=True, vmem_limit_bytes=56 * 2**20
        ),
    )(
        valid, ln1_gain.reshape(1, D), ln2_gain.reshape(1, D),
        frames, w_query, w_key, w_value, w_out, w_up, w_down,
    )


def solution(mesh):
    placed = (
        P(None, "tm", None),
        P(),
        P(),
        P(None, "mp"),
        P(None, "mp"),
        P(None, "mp"),
        P("mp", None),
        P(),
        P(None, "mp"),
        P("mp", None),
    )
    return jax.shard_map(
        body, mesh=mesh, in_specs=placed, out_specs=P(None, "tm", "mp"), check_vma=False
    )
```

time: 124 us -> 99.4 us (0.80)
  Pallas kernels: 122 us -> 97.3 us
    pallas_call x1, Pallas kernels: 122 us -> 97.3 us  [body(): pl.pallas_call(kernel, name='layer', out_shape=jax.ShapeDtypeStruct((fram...]
where the time goes in v1:
time: 99.4 us; the launch traced here: 99.3 us
  Pallas kernels  97.3 us (98%)
  local copies, waits for them, and re-layouts  1.97 us (2%)
    pallas_call x1, Pallas kernels, body(): pl.pallas_call(kernel, name='layer', out_shape=jax.ShapeDtypeStruct((fram...  97.3 us

profile of v1, /device:TPU:1, one launch (start us, length us, event | category | flops | bytes accessed | tf_op | source)
XLA Modules:
  0.0 99.3 jit_solution(8572970631973204601)
XLA Ops:
  0.0 97.3 %layer.1 = bf16[4,640,128]{2,1,0:T(8,128)(2,1)} custom-call(s32[4]{0:T(128)} %valid.1, f32[1,1024]{1,0:T(1,128)} %bitcast.2, f32[1,1024]{1,0:T(1,128)} %bitcast.3, bf16[4,640,1024]{2,1,0:T(8,128)(2,1)} %frames.1, bf16[1024,128]{1,0:T(8,128)(2,1)} %wq.1, bf16[1024,128]{1,0:T(8,128)(2,1)} %wk.1, bf16[1024,128]{1,0:T(8,128)(2,1)} %wv.1, bf16[128,1024]{1,0:T(8,128)(2,1)} %wo.1, ...), custom_call_target="tpu_custom_call" | custom-call | tf_op jit(solution)/shard_map/layer/pallas_call | solution.py:621
  97.3 2.0 %copy.12 = bf16[4,640,128]{2,1,0:T(8,128)(2,1)} copy(bf16[4,640,128]{2,1,0:T(8,128)(2,1)} %layer.1) | data formatting | bytes 1310720

commit v2 on v1

v2 whole, which is shorter than its diff:
```python
import jax
import jax.numpy as jnp
from jax import lax
from jax.experimental import pallas as pl
from jax.experimental.pallas import tpu as pltpu
from jax.sharding import PartitionSpec as P

MESH = pl.DeviceIdType.MESH
F32 = jnp.float32
BF16 = jnp.bfloat16

D = 1024
SEG = 160
LOOK = 32
KEYS = SEG + LOOK
OWN = 2 * SEG
SPAN = 4 * SEG
SLOTS = 128
EPS = 1e-05
NEG = -1e30
N_SEM = 192

SCHEDULE = (
    "pre0 pre2 pre4 pre6",
    "enter u0:0 wo:0 u1:0",
    "look pre1 pre3 pre5",
    "d2:0 pre7 u0:1 d1:0",
    "turns wo:1 u0:2 u1:1",
    "d2:1 d1:1 d3:0 d0:0",
    "summary wo:2 u0:3 d3:1",
    "d0:1 u1:2 near20 d2:2",
    "near21 d1:2 near10 wo:3",
    "memory u0:4 near11 near30",
    "d3:2 d0:2 near31 near01",
    "u1:3 d2:3 d1:3 d3:3",
    "bank_b near00 d0:3 u1:4",
    "bank_c far20 d2:4 far21",
    "far10 far11 d1:4 far30",
    "far31 far01 d3:4 far00",
    "d0:4 mix norm_two up00",
    "up01 u0:5 up02 up03",
    "up10 up11 u1:5 up12",
    "up13 d2:5 down2 d1:5",
    "down1 d3:5 down3 d0:5",
    "down0",
)


def dot(a, b):
    return jnp.dot(a, b, preferred_element_type=F32)


def normalize(x, gain):
    mean = jnp.sum(x, -1, keepdims=True) * (1.0 / D)
    square = jnp.sum(x * x, -1, keepdims=True) * (1.0 / D)
    return (x - mean) * lax.rsqrt(square - mean * mean + EPS) * gain


def kernel(
    valid, g1, g2, frames, wq, wk, wv, wo, up, dn, out,
    xs, nrm, wqkv, sums, qb, kb, vb, kt, look_out, look_in, so_all, bank, memf, bk, bv,
    wo_b, up_b, dn_b, acc, mx, fo_out, fo_in, mixed, n2, hid, ob,
    loc_sem, send_sem, recv_sem,
):
    tm = lax.axis_index("tm")
    mp = lax.axis_index("mp")
    x = tm // 8
    y = (tm // 2) % 4
    zl = mp // 2
    z = (tm % 2) * 4 + zl
    c = mp % 2
    valid_at = lambda which: valid[which] - tm * SPAN

    def dev(px, py, pz, pc):
        return ((px * 4 + py) * 2 + pz // 4, (pz % 4) * 2 + pc)

    def z_dev(step):
        return dev(x, y, (z + step + 8) % 8, c)

    sibling = (tm, zl * 2 + 1 - c)

    barrier = pltpu.get_barrier_semaphore()

    before, after = ((tm + 31) % 32, mp), ((tm + 1) % 32, mp)
    greeted = [before, after] + [z_dev(step) for step in (1, -1, 2, -2)]
    greeted += [(tm, (mp + i) % 8) for i in range(1, 8)]
    bank_one = [dev((x + i) % 4, y, (z + j) % 8, c) for j in (4, 0) for i in (2, 1, 3, 0) if i or j]
    bank_two = [dev(x, (y + i) % 4, z, c) for i in (2, 1, 3)]
    greeted += bank_one + bank_two
    for other in greeted:
        pl.semaphore_signal(barrier, inc=1, device_id=other, device_id_type=MESH)

    used = [0]
    sent = []

    def remote(src, dst, to):
        i = used[0]
        used[0] += 1
        copy = pltpu.make_async_remote_copy(
            src_ref=src, dst_ref=dst, send_sem=send_sem.at[i], recv_sem=recv_sem.at[i],
            device_id=to, device_id_type=MESH,
        )
        sent.append(copy)
        copy.start()
        return copy

    n_local = [0]

    def local(src, dst):
        i = n_local[0]
        n_local[0] += 1
        copy = pltpu.make_async_copy(src, dst, loc_sem.at[i])
        copy.start()
        return copy

    xs_copies = [local(frames.at[b], xs.at[b]) for b in range(4)]
    w_copies = [
        local(ref, wqkv.at[:, pl.ds(i * 128, 128)]) for i, ref in enumerate((wq, wk, wv))
    ]
    own_copies = [local(wo, wo_b.at[0, 0])]
    for j in range(2):
        own_copies.append(local(up.at[:, pl.ds(j * 256, 256)], up_b.at[j, 0, 0]))

    def q_cols(step):
        return pl.ds(pl.multiple_of(((zl + step) % 4) * 256, 256), 256)

    for r in range(4):
        own_copies.append(local(dn.at[:, q_cols(r)], dn_b.at[r, 0, 0]))

    lx = (x + c) % 4
    ly = (y + c) % 4

    def at_x(label):
        return dev((label + 4 - c) % 4, y, z, c)

    def at_y(label):
        return dev(x, (label + 4 - c) % 4, z, c)

    def first(label):
        return label + 1 - 2 * (label % 2)

    def second(label):
        return 3 - label

    class Half:
        def __init__(self, kind, source, view, base, rows):
            self.source, self.view, self.base, self.rows = source, view, base, rows
            if kind == 0:
                self.a, self.b, self.at_a, self.at_b = lx, ly, at_x, at_y
            else:
                self.a, self.b, self.at_a, self.at_b = ly, lx, at_y, at_x
            self.far = 2 if kind == 0 else -2

        def span(self, index, count):
            return pl.ds(pl.multiple_of(self.base + index * self.rows, self.rows), count * self.rows)

        def z(self):
            here = self.span(self.b * 4 + self.a, 1)
            self.arrive = [
                remote(self.source(1, here), self.view(0, pl.ds(3, 1), here), z_dev(1)),
                remote(self.source(-1, here), self.view(0, pl.ds(1, 1), here), z_dev(-1)),
                remote(self.source(self.far, here), self.view(0, pl.ds(2, 1), here), z_dev(self.far)),
            ]

        def hop(self, rows, to):
            for copy in self.arrive:
                copy.wait_recv()
            part = self.view(0, pl.ds(1, 3), rows)
            self.arrive = [remote(part, part, to)]

        def s1(self):
            for copy in self.arrive:
                copy.wait_recv()
            part = self.view(0, pl.ds(1, 3), self.span(self.b * 4 + self.a, 1))
            self.arrive = [remote(part, part, self.at_a((self.a + i) % 4)) for i in (2, 1, 3)]

        def s2(self):
            self.hop(self.span(self.b * 4, 4), self.at_b(first(self.b)))

        def s3(self):
            near = self.span(8 * (self.b // 2), 8)
            self.hop(near, self.at_b(second(self.b)))
            self.share = [
                remote(self.view(0, pl.ds(1, 3), near), self.view(1, pl.ds(1, 3), near), sibling)
            ]

        def s4(self):
            for copy in self.arrive:
                copy.wait_recv()
            rest = self.span(8 - 8 * (self.b // 2), 8)
            self.share.append(
                remote(self.view(0, pl.ds(1, 3), rest), self.view(1, pl.ds(1, 3), rest), sibling)
            )

        def s5(self):
            for copy in self.share:
                copy.wait_recv()

    class Group:
        def __init__(self, halves, own, own_src):
            self.halves = halves
            self.own, self.own_src = own, own_src

        def z(self):
            for half in self.halves:
                half.z()
            self.own_copies = [
                remote(src, dst.at[pl.ds(1, 1), pl.ds(0, 1)], sibling)
                for src, dst in zip(self.own_src, self.own)
            ]

        def run(self, stage):
            if stage == 0:
                return self.z()
            for half in self.halves:
                getattr(half, "s%d" % stage)()
            if stage == 5:
                for copy in self.own_copies:
                    copy.wait_recv()

    def four(ref, rows, columns):
        return ref.reshape(1, 1, rows, columns)

    def half_up(kind, j):
        return Half(
            kind,
            lambda step, rows: four(up, D, 512).at[0, :, rows, pl.ds(j * 256, 256)],
            lambda e, d, rows: up_b.at[j, e, d, rows, :],
            kind * 512, 32,
        )

    def half_dn(kind, r):
        return Half(
            kind,
            lambda step, rows: four(dn, 512, D).at[0, :, rows, q_cols(r + step + 4)],
            lambda e, d, rows: dn_b.at[r, e, d, rows, :],
            kind * 256, 16,
        )

    groups = {}
    for j in range(2):
        groups["u%d" % j] = Group(
            [half_up(0, j), half_up(1, j)], [up_b.at[j]],
            [four(up, D, 512).at[:, :, :, pl.ds(j * 256, 256)]],
        )
    for r in range(4):
        groups["d%d" % r] = Group(
            [half_dn(0, r), half_dn(1, r)], [dn_b.at[r]],
            [four(dn, 512, D).at[:, :, :, q_cols(r)]],
        )

    class Ring:
        def __init__(self, ref, buf, rows):
            self.ref, self.buf, self.rows = ref, buf, rows

        def run(self, stage):
            buf, half = self.buf, self.rows // 2
            if stage == 0:
                self.up = remote(self.ref, buf.at[0, 3], z_dev(1))
                self.down = remote(self.ref, buf.at[0, 1], z_dev(-1))
                self.share = [remote(self.ref, buf.at[1, 0], sibling)]
            elif stage == 1:
                self.up.wait_recv()
                self.down.wait_recv()
                high, low = pl.ds(half, half), pl.ds(0, half)
                self.far = [
                    remote(buf.at[0, 3, high], buf.at[0, 2, high], z_dev(1)),
                    remote(buf.at[0, 1, low], buf.at[0, 2, low], z_dev(-1)),
                ]
                self.share.append(remote(buf.at[0, 1], buf.at[1, 1], sibling))
                self.share.append(remote(buf.at[0, 3], buf.at[1, 3], sibling))
            elif stage == 2:
                for copy in self.far:
                    copy.wait_recv()
                self.share.append(remote(buf.at[0, 2], buf.at[1, 2], sibling))
            else:
                for copy in self.share:
                    copy.wait_recv()

    groups["wo"] = Ring(wo, wo_b, 128)

    acts = {}

    def action(f):
        acts[f.__name__] = f
        return f

    def loop(f, lo, hi, unroll=1):
        lax.fori_loop(lo, hi, lambda i, carry: (f(i), carry)[1], 0, unroll=unroll)

    @action
    def enter():
        pl.semaphore_wait(barrier, len(greeted))

    held = {}

    def pre(n):
        b, half = n // 2, n % 2
        if n == 0:
            for copy in w_copies:
                copy.wait()
        if half == 0:
            xs_copies[b].wait()

        def norm_rows(i):
            rows = pl.ds(pl.multiple_of(half * OWN + i * 32, 32), 32)
            here = pl.ds(pl.multiple_of(i * 32, 32), 32)
            nrm[n % 2, here, :] = normalize(xs[b, rows, :].astype(F32), g1[...]).astype(BF16)

        loop(norm_rows, 0, 10, unroll=2)
        normed = nrm[n % 2]
        got = dot(normed, wqkv[...])
        rows = slice(half * OWN, half * OWN + OWN)
        qb[b, rows] = got[:, :128].astype(BF16) * jnp.asarray(0.125, BF16)
        kb[b, rows] = got[:, 128:256]
        vb[b, rows] = got[:, 256:].astype(BF16)
        if half == 0:
            look_out[b] = got[:LOOK, 128:].astype(BF16)
        row_i = lax.broadcasted_iota(jnp.int32, (16, OWN), 0)
        col_i = lax.broadcasted_iota(jnp.int32, (16, OWN), 1)
        live = col_i < valid_at(b) - half * OWN
        inside = (col_i >= row_i * SEG) & (col_i < row_i * SEG + SEG) & live
        picks = jnp.where(inside, 1.0, 0.0)
        counts = jnp.sum(picks, -1, keepdims=True)
        total = dot(picks.astype(BF16), normed) / jnp.maximum(counts, 1.0)
        sums[2 * n : 2 * n + 2, :] = total[:2]

    for n in range(8):
        acts["pre%d" % n] = lambda n=n: pre(n)

    @action
    def look():
        held["look"] = remote(look_out, look_in, before)

    def turn(b):
        for sl in range(4):
            kt[b * 4 + sl] = kb[b, sl * SEG : sl * SEG + KEYS].T.astype(BF16)

    @action
    def turns():
        held["look"].wait_recv()
        for b in range(4):
            kb[b, SPAN:] = look_in[b, :, :128].astype(F32)
            vb[b, SPAN:] = look_in[b, :, 128:]
        for copy in own_copies:
            copy.wait()
        loop(turn, 0, 4)

    @action
    def summary():
        asked = dot(sums[...].astype(BF16), wqkv[:, :128]).astype(BF16).astype(F32) * 0.125
        row = lax.broadcasted_iota(jnp.int32, (8, 128), 0)
        head = lax.broadcasted_iota(jnp.int32, (8, 128), 1) // 64
        key_l = lax.broadcasted_iota(jnp.int32, (8, KEYS), 1)
        parts = []
        for g in range(16):
            q = jnp.where(row == head, jnp.broadcast_to(asked[g : g + 1], (8, 128)), 0.0)
            score = dot(q.astype(BF16), kt[g])
            parts.append(jnp.where(key_l < valid_at(g // 4) - (g % 4) * SEG, score, NEG))
        scores = jnp.concatenate(parts, axis=0)
        p = jnp.exp(scores - jnp.max(scores, -1, keepdims=True))
        p = p / jnp.sum(p, -1, keepdims=True)
        parts = []
        for g in range(16):
            at = (g % 4) * SEG
            got = dot(p[g * 8 : g * 8 + 8].astype(BF16), vb[g // 4, at : at + KEYS, :])
            parts.append(jnp.where(head[:1] == 0, got[0:1], got[1:2]))
        so_all[0, 0] = jnp.concatenate(parts, axis=0).astype(BF16)
        held["so"] = []
        for dz in (2, 3, 1, 0):
            for e in range(2):
                if dz or e:
                    to = (tm, ((zl + dz) % 4) * 2 + (c if e == 0 else 1 - c))
                    held["so"].append(remote(so_all.at[0, 0], so_all.at[e, (4 - dz) % 4], to))

    zh = tm % 2

    @action
    def memory():
        for copy in held["so"]:
            copy.wait_recv()
        summed = jnp.concatenate([so_all[e, d] for e in range(2) for d in range(4)], axis=1)
        got = dot(summed, wo_b[...].reshape(D, D)).astype(BF16)
        bank[x, y, zh] = dot(got, wqkv[:, 128:]).astype(BF16)
        part = bank.at[x, y, zh]
        held["bank"] = [remote(part, part, other) for other in bank_one]

    @action
    def bank_b():
        for copy in held["bank"]:
            copy.wait_recv()
        part = bank.at[:, pl.ds(y, 1)]
        held["bank"] = [remote(part, part, other) for other in bank_two]

    @action
    def bank_c():
        for copy in held["bank"]:
            copy.wait_recv()
        memf[0] = bank[:, :, :, :, :128].reshape(SLOTS * 4, 128).astype(F32)
        memf[1] = bank[:, :, :, :, 128:].reshape(SLOTS * 4, 128).astype(F32)
        for b in range(4):
            both = [
                jnp.concatenate(
                    [memf[i, pl.ds(b * 4 + sl, 32, stride=16), :] for sl in range(4)], axis=0
                )
                for i in range(2)
            ]
            bk[b] = both[0].T.astype(BF16)
            bv[b] = both[1].astype(BF16)

    lane = lax.broadcasted_iota(jnp.int32, (SEG, 128), 1)

    def one_head(b, seg, h):
        q = qb[b, pl.ds(pl.multiple_of(seg * SEG, 32), SEG), :]
        mine = lane < 64 if h == 0 else lane >= 64
        return jnp.where(mine, q, jnp.zeros_like(q))

    def with_ones(v):
        return jnp.concatenate([v, jnp.ones_like(v)], axis=1)

    def near_step(b, seg):
        g = b * 4 + seg
        near_l = lax.broadcasted_iota(jnp.int32, (SEG, KEYS), 1)
        ones = with_ones(vb[b, pl.ds(pl.multiple_of(seg * SEG, 32), KEYS), :])
        for h in range(2):
            near = dot(one_head(b, seg, h), kt[g])
            near = jnp.where(near_l < valid_at(b) - seg * SEG, near, NEG)
            top = jnp.max(near, -1, keepdims=True)
            near = jnp.exp(near - top).astype(BF16)
            rows = slice(h * SEG, h * SEG + SEG)
            acc[g, rows] = dot(near, ones)
            mx[g, rows] = jnp.broadcast_to(top, (SEG, 128))

    def far_step(b, seg, s, dest):
        g = b * 4 + seg
        far_l = lax.broadcasted_iota(jnp.int32, (SEG, SLOTS), 1)
        far_l = (far_l % 32) * 4 + far_l // 32
        far_ok = (far_l < tm * 4 + seg) & (far_l * SEG < valid[b])
        both = []
        for h in range(2):
            rows = slice(h * SEG, h * SEG + SEG)
            far = jnp.where(far_ok, dot(one_head(b, seg, h), bk[b]), NEG)
            before = mx[g, rows]
            top = jnp.maximum(before, jnp.max(far, -1, keepdims=True))
            far = jnp.exp(far - top).astype(BF16)
            keep = jnp.exp(before - top)
            got = dot(far, with_ones(bv[b]))
            total = acc[g, rows, 128:] * keep + got[:, 128:]
            both.append((acc[g, rows, :128] * keep + got[:, :128]) / total)
        dest[s * SEG : s * SEG + SEG, :] = jnp.where(lane < 64, both[0], both[1]).astype(BF16)

    def place(r, i):
        return (zl + r) % 4, (c if i == 0 else 1 - c)

    def near(r, i):
        b, core = place(r, i)
        for s in range(2):
            near_step(b, core * 2 + s)

    held["fo"] = []

    def far(r, i):
        b, core = place(r, i)
        dest = fo_out.at[r, i] if r or i else fo_in.at[0, 0]
        for s in range(2):
            far_step(b, core * 2 + s, s, dest)
        if r or i:
            held["fo"].append(remote(dest, fo_in.at[i, (4 - r) % 4], (tm, b * 2 + core)))

    for r in range(4):
        for i in range(2):
            acts["near%d%d" % (r, i)] = lambda r=r, i=i: near(r, i)
            acts["far%d%d" % (r, i)] = lambda r=r, i=i: far(r, i)

    @action
    def mix():
        for copy in held["fo"]:
            copy.wait_recv()
        rows = jnp.concatenate([fo_in[e, d] for e in range(2) for d in range(4)], axis=1)
        own = pl.ds(pl.multiple_of(c * OWN, OWN), OWN)
        for n in range(4):
            weight = wo_b[:, :, :, n * 256 : n * 256 + 256].reshape(D, 256)
            mixed[n] = dot(rows, weight) + xs[zl, own, n * 256 : n * 256 + 256].astype(F32)

    @action
    def norm_two():
        def step(i):
            rows = pl.ds(pl.multiple_of(i * 32, 32), 32)
            v = jnp.concatenate([mixed[n, rows, :] for n in range(4)], axis=1)
            n2[rows, :] = normalize(v, g2[...]).astype(BF16)

        loop(step, 0, 10, unroll=2)

    def up_step(j, b):
        h = dot(n2[...], up_b[j, b // 4, b % 4])
        h = 0.5 * h * (1.0 + lax.erf(h * (2.0 ** -0.5)))
        hid[:, pl.ds(pl.multiple_of(b * 512 + j * 256, 256), 256)] = h.astype(BF16)

    for j in range(2):
        for k in range(4):
            acts["up%d%d" % (j, k)] = lambda j=j, k=k: loop(
                lambda b: up_step(j, b), 2 * k, 2 * k + 2)

    outs = []
    row_span = pl.ds(pl.multiple_of(c * OWN, OWN), OWN)

    def down(r):
        block = dot(hid[...], dn_b[r].reshape(4 * D, 256))
        to = (zl + r) % 4
        block = (block + mixed[to]).astype(BF16)
        ob[r, 0] = block[:, :128]
        ob[r, 1] = block[:, 128:]
        if r:
            for core in (c, 1 - c):
                outs.append(remote(ob.at[r, core], out.at[zl, row_span, :], (tm, to * 2 + core)))
        else:
            outs.append(remote(ob.at[0, 1 - c], out.at[zl, row_span, :], sibling))
            held["home"] = local(ob.at[0, c], out.at[zl, row_span, :])

    for r in range(4):
        acts["down%d" % r] = lambda r=r: down(r)

    for token in " ".join(SCHEDULE).split():
        if ":" in token:
            name, stage = token.split(":")
            groups[name].run(int(stage))
        else:
            acts[token]()
    held["home"].wait()
    for copy in outs:
        copy.wait_recv()
    for copy in sent:
        copy.wait_send()
    assert used[0] <= N_SEM, used[0]


def body(frames, valid, ln1_gain, w_query, w_key, w_value, w_out, ln2_gain, w_up, w_down):
    vmem = pl.BlockSpec(memory_space=pltpu.VMEM)
    anywhere = pl.BlockSpec(memory_space=pl.ANY)
    scratch = [
        pltpu.VMEM((4, SPAN, D), BF16),
        pltpu.VMEM((2, OWN, D), BF16),
        pltpu.VMEM((D, 384), BF16),
        pltpu.VMEM((16, D), F32),
        pltpu.VMEM((4, SPAN, 128), BF16),
        pltpu.VMEM((4, SPAN + LOOK, 128), F32),
        pltpu.VMEM((4, SPAN + LOOK, 128), BF16),
        pltpu.VMEM((16, 128, KEYS), BF16),
        pltpu.VMEM((4, LOOK, 256), BF16),
        pltpu.VMEM((4, LOOK, 256), BF16),
        pltpu.VMEM((2, 4, 16, 128), BF16),
        pltpu.VMEM((4, 4, 2, 16, 256), BF16),
        pltpu.VMEM((2, SLOTS * 4, 128), F32),
        pltpu.VMEM((4, 128, SLOTS), BF16),
        pltpu.VMEM((4, SLOTS, 128), BF16),
        pltpu.VMEM((2, 4, 128, D), BF16),
        pltpu.VMEM((2, 2, 4, D, 256), BF16),
        pltpu.VMEM((4, 2, 4, 512, 256), BF16),
        pltpu.VMEM((16, OWN, 256), F32),
        pltpu.VMEM((16, OWN, 128), F32),
        pltpu.VMEM((4, 2, OWN, 128), BF16),
        pltpu.VMEM((2, 4, OWN, 128), BF16),
        pltpu.VMEM((4, OWN, 256), F32),
        pltpu.VMEM((OWN, D), BF16),
        pltpu.VMEM((OWN, 4 * D), BF16),
        pltpu.VMEM((4, 2, OWN, 128), BF16),
        pltpu.SemaphoreType.DMA((16,)),
        pltpu.SemaphoreType.DMA((N_SEM,)),
        pltpu.SemaphoreType.DMA((N_SEM,)),
    ]
    return pl.pallas_call(
        kernel,
        name="layer",
        out_shape=jax.ShapeDtypeStruct((frames.shape[0], frames.shape[1], 128), BF16),
        in_specs=[pl.BlockSpec(memory_space=pltpu.SMEM), vmem, vmem] + [anywhere] * 7,
        out_specs=anywhere,
        scratch_shapes=scratch,
        compiler_params=pltpu.CompilerParams(
            collective_id=0, has_side_effects=True, vmem_limit_bytes=56 * 2**20
        ),
    )(
        valid, ln1_gain.reshape(1, D), ln2_gain.reshape(1, D),
        frames, w_query, w_key, w_value, w_out, w_up, w_down,
    )


def solution(mesh):
    placed = (
        P(None, "tm", None),
        P(),
        P(),
        P(None, "mp"),
        P(None, "mp"),
        P(None, "mp"),
        P("mp", None),
        P(),
        P(None, "mp"),
        P("mp", None),
    )
    return jax.shard_map(
        body, mesh=mesh, in_specs=placed, out_specs=P(None, "tm", "mp"), check_vma=False
    )
```

time: 99.4 us -> 112 us (1.13)
  Pallas kernels: 97.3 us -> 110 us
    pallas_call x1, Pallas kernels: 97.3 us -> 110 us  [body(): pl.pallas_call(kernel, name='layer', out_shape=jax.ShapeDtypeStruct((fram...]
where the time goes in v2:
time: 112 us
  Pallas kernels  110 us (98%)
  local copies, waits for them, and re-layouts  1.97 us (2%)
    pallas_call x1, Pallas kernels, body(): pl.pallas_call(kernel, name='layer', out_shape=jax.ShapeDtypeStruct((fram...  110 us

profile of v2, /device:TPU:1, one launch (start us, length us, event | category | flops | bytes accessed | tf_op | source)
XLA Modules:
  0.0 111.8 jit_solution(14614142385161440147)
XLA Ops:
  0.0 109.8 %layer.1 = bf16[4,640,128]{2,1,0:T(8,128)(2,1)} custom-call(s32[4]{0:T(128)} %valid.1, f32[1,1024]{1,0:T(1,128)} %bitcast.2, f32[1,1024]{1,0:T(1,128)} %bitcast.3, bf16[4,640,1024]{2,1,0:T(8,128)(2,1)} %frames.1, bf16[1024,128]{1,0:T(8,128)(2,1)} %wq.1, bf16[1024,128]{1,0:T(8,128)(2,1)} %wk.1, bf16[1024,128]{1,0:T(8,128)(2,1)} %wv.1, bf16[128,1024]{1,0:T(8,128)(2,1)} %wo.1, ...), custom_call_target="tpu_custom_call" | custom-call | tf_op jit(solution)/shard_map/layer/pallas_call | solution.py:571
  109.8 2.0 %copy.12 = bf16[4,640,128]{2,1,0:T(8,128)(2,1)} copy(bf16[4,640,128]{2,1,0:T(8,128)(2,1)} %layer.1) | data formatting | bytes 1310720

commit v3 on v2

--- a/solution.py
+++ b/solution.py
@@ -22,27 +22,32 @@
 
 SCHEDULE = (
     "pre0 pre2 pre4 pre6",
-    "enter u0:0 wo:0 u1:0",
-    "look pre1 pre3 pre5",
-    "d2:0 pre7 u0:1 d1:0",
-    "turns wo:1 u0:2 u1:1",
-    "d2:1 d1:1 d3:0 d0:0",
-    "summary wo:2 u0:3 d3:1",
-    "d0:1 u1:2 near20 d2:2",
-    "near21 d1:2 near10 wo:3",
-    "memory u0:4 near11 near30",
-    "d3:2 d0:2 near31 near01",
-    "u1:3 d2:3 d1:3 d3:3",
-    "bank_b near00 d0:3 u1:4",
-    "bank_c far20 d2:4 far21",
-    "far10 far11 d1:4 far30",
-    "far31 far01 d3:4 far00",
-    "d0:4 mix norm_two up00",
-    "up01 u0:5 up02 up03",
-    "up10 up11 u1:5 up12",
-    "up13 d2:5 down2 d1:5",
-    "down1 d3:5 down3 d0:5",
-    "down0",
+    "enter u0:0 wo:0 look",
+    "pre1 pre3 u1:0 pre5",
+    "pre7 d2:0 wo:1 u0:1",
+    "turns summary near20 d1:0",
+    "wo:2 near21 near10 near11",
+    "u1:1 d2:1 d3:0 wo:3",
+    "memory u0:2 near30 d0:0",
+    "near31 d1:1 near01 u1:2",
+    "d3:1 bank_b d2:2 near00",
+    "u0:3 d0:1 d1:2 bank_c",
+    "far200 far210 far100 far110",
+    "u1:3 far300 far310 far010",
+    "d3:2 far000 d2:3 far201",
+    "far211 far101 far111 far301",
+    "far311 far011 far001 u0:4",
+    "d0:2 d1:3 mix0 norm0",
+    "u1:4 up000 up010 d3:3",
+    "u0:5 up020 up030 up100",
+    "d2:4 up110 u1:5 up120",
+    "d0:3 up130 d2:5 down20",
+    "d1:4 d1:5 down10 d3:4",
+    "d3:5 down30 d0:4 d0:5",
+    "down00 mix1 norm1 up001",
+    "up011 up021 up031 up101",
+    "up111 up121 up131 down21",
+    "down11 down31 down01",
 )
 
 
@@ -431,7 +436,7 @@
             acc[g, rows] = dot(near, ones)
             mx[g, rows] = jnp.broadcast_to(top, (SEG, 128))
 
-    def far_step(b, seg, s, dest):
+    def far_step(b, seg, dest):
         g = b * 4 + seg
         far_l = lax.broadcasted_iota(jnp.int32, (SEG, SLOTS), 1)
         far_l = (far_l % 32) * 4 + far_l // 32
@@ -447,7 +452,7 @@
             got = dot(far, with_ones(bv[b]))
             total = acc[g, rows, 128:] * keep + got[:, 128:]
             both.append((acc[g, rows, :128] * keep + got[:, :128]) / total)
-        dest[s * SEG : s * SEG + SEG, :] = jnp.where(lane < 64, both[0], both[1]).astype(BF16)
+        dest[...] = jnp.where(lane < 64, both[0], both[1]).astype(BF16)
 
     def place(r, i):
         return (zl + r) % 4, (c if i == 0 else 1 - c)
@@ -457,68 +462,79 @@
         for s in range(2):
             near_step(b, core * 2 + s)
 
-    held["fo"] = []
-
-    def far(r, i):
+    held["fo"] = [[], []]
+
+    def far(r, i, s):
         b, core = place(r, i)
-        dest = fo_out.at[r, i] if r or i else fo_in.at[0, 0]
-        for s in range(2):
-            far_step(b, core * 2 + s, s, dest)
+        rows = pl.ds(s * SEG, SEG)
         if r or i:
-            held["fo"].append(remote(dest, fo_in.at[i, (4 - r) % 4], (tm, b * 2 + core)))
+            dest = fo_out.at[r, i, rows]
+            far_step(b, core * 2 + s, dest)
+            there = fo_in.at[i, (4 - r) % 4, rows]
+            held["fo"][s].append(remote(dest, there, (tm, b * 2 + core)))
+        else:
+            far_step(b, core * 2 + s, fo_in.at[0, 0, rows])
 
     for r in range(4):
         for i in range(2):
             acts["near%d%d" % (r, i)] = lambda r=r, i=i: near(r, i)
-            acts["far%d%d" % (r, i)] = lambda r=r, i=i: far(r, i)
-
-    @action
-    def mix():
-        for copy in held["fo"]:
+            for s in range(2):
+                acts["far%d%d%d" % (r, i, s)] = lambda r=r, i=i, s=s: far(r, i, s)
+
+    def mix(s):
+        for copy in held["fo"][s]:
             copy.wait_recv()
-        rows = jnp.concatenate([fo_in[e, d] for e in range(2) for d in range(4)], axis=1)
-        own = pl.ds(pl.multiple_of(c * OWN, OWN), OWN)
+        part = slice(s * SEG, s * SEG + SEG)
+        rows = jnp.concatenate([fo_in[e, d, part] for e in range(2) for d in range(4)], axis=1)
+        own = pl.ds(pl.multiple_of(c * OWN + s * SEG, 32), SEG)
         for n in range(4):
             weight = wo_b[:, :, :, n * 256 : n * 256 + 256].reshape(D, 256)
-            mixed[n] = dot(rows, weight) + xs[zl, own, n * 256 : n * 256 + 256].astype(F32)
-
-    @action
-    def norm_two():
+            mixed[n, part] = dot(rows, weight) + xs[zl, own, n * 256 : n * 256 + 256].astype(F32)
+
+    def norm_two(s):
         def step(i):
-            rows = pl.ds(pl.multiple_of(i * 32, 32), 32)
+            rows = pl.ds(pl.multiple_of(s * SEG + i * 32, 32), 32)
             v = jnp.concatenate([mixed[n, rows, :] for n in range(4)], axis=1)
             n2[rows, :] = normalize(v, g2[...]).astype(BF16)
 
-        loop(step, 0, 10, unroll=2)
-
-    def up_step(j, b):
-        h = dot(n2[...], up_b[j, b // 4, b % 4])
+        loop(step, 0, 5)
+
+    def up_step(j, b, s):
+        part = slice(s * SEG, s * SEG + SEG)
+        h = dot(n2[part, :], up_b[j, b // 4, b % 4])
         h = 0.5 * h * (1.0 + lax.erf(h * (2.0 ** -0.5)))
-        hid[:, pl.ds(pl.multiple_of(b * 512 + j * 256, 256), 256)] = h.astype(BF16)
-
-    for j in range(2):
-        for k in range(4):
-            acts["up%d%d" % (j, k)] = lambda j=j, k=k: loop(
-                lambda b: up_step(j, b), 2 * k, 2 * k + 2)
+        hid[part, pl.ds(pl.multiple_of(b * 512 + j * 256, 256), 256)] = h.astype(BF16)
+
+    for s in range(2):
+        acts["mix%d" % s] = lambda s=s: mix(s)
+        acts["norm%d" % s] = lambda s=s: norm_two(s)
+        for j in range(2):
+            for k in range(4):
+                acts["up%d%d%d" % (j, k, s)] = lambda j=j, k=k, s=s: loop(
+                    lambda b: up_step(j, b, s), 2 * k, 2 * k + 2, unroll=2)
 
     outs = []
-    row_span = pl.ds(pl.multiple_of(c * OWN, OWN), OWN)
-
-    def down(r):
-        block = dot(hid[...], dn_b[r].reshape(4 * D, 256))
+    held["home"] = []
+
+    def down(r, s):
+        part = slice(s * SEG, s * SEG + SEG)
+        rows = pl.ds(s * SEG, SEG)
+        there = out.at[zl, pl.ds(pl.multiple_of(c * OWN + s * SEG, 32), SEG), :]
+        block = dot(hid[part, :], dn_b[r].reshape(4 * D, 256))
         to = (zl + r) % 4
-        block = (block + mixed[to]).astype(BF16)
-        ob[r, 0] = block[:, :128]
-        ob[r, 1] = block[:, 128:]
+        block = (block + mixed[to, part]).astype(BF16)
+        ob[r, 0, part] = block[:, :128]
+        ob[r, 1, part] = block[:, 128:]
         if r:
             for core in (c, 1 - c):
-                outs.append(remote(ob.at[r, core], out.at[zl, row_span, :], (tm, to * 2 + core)))
+                outs.append(remote(ob.at[r, core, rows], there, (tm, to * 2 + core)))
         else:
-            outs.append(remote(ob.at[0, 1 - c], out.at[zl, row_span, :], sibling))
-            held["home"] = local(ob.at[0, c], out.at[zl, row_span, :])
+            outs.append(remote(ob.at[0, 1 - c, rows], there, sibling))
+            held["home"].append(local(ob.at[0, c, rows], there))
 
     for r in range(4):
-        acts["down%d" % r] = lambda r=r: down(r)
+        for s in range(2):
+            acts["down%d%d" % (r, s)] = lambda r=r, s=s: down(r, s)
 
     for token in " ".join(SCHEDULE).split():
         if ":" in token:
@@ -526,7 +542,8 @@
             groups[name].run(int(stage))
         else:
             acts[token]()
-    held["home"].wait()
+    for copy in held["home"]:
+        copy.wait()
     for copy in outs:
         copy.wait_recv()
     for copy in sent:

time: 112 us -> 89.9 us (0.80)
  Pallas kernels: 110 us -> 87.5 us
    pallas_call x1, Pallas kernels: 110 us -> 87.5 us  [body(): pl.pallas_call(kernel, name='layer', out_shape=jax.ShapeDtypeStruct((fram...]
where the time goes in v3:
time: 89.9 us; the launch traced here: 89.5 us
  Pallas kernels  87.5 us (97%)
  local copies, waits for them, and re-layouts  1.97 us (2%)
    pallas_call x1, Pallas kernels, body(): pl.pallas_call(kernel, name='layer', out_shape=jax.ShapeDtypeStruct((fram...  87.5 us
    unnamed x1, local copies, waits for them, and re-layouts  1.97 us

profile of v3, /device:TPU:1, one launch (start us, length us, event | category | flops | bytes accessed | tf_op | source)
XLA Modules:
  0.0 89.5 jit_solution(17654313941064156894)
XLA Ops:
  0.0 87.5 %layer.1 = bf16[4,640,128]{2,1,0:T(8,128)(2,1)} custom-call(s32[4]{0:T(128)} %valid.1, f32[1,1024]{1,0:T(1,128)} %bitcast.2, f32[1,1024]{1,0:T(1,128)} %bitcast.3, bf16[4,640,1024]{2,1,0:T(8,128)(2,1)} %frames.1, bf16[1024,128]{1,0:T(8,128)(2,1)} %wq.1, bf16[1024,128]{1,0:T(8,128)(2,1)} %wk.1, bf16[1024,128]{1,0:T(8,128)(2,1)} %wv.1, bf16[128,1024]{1,0:T(8,128)(2,1)} %wo.1, ...), custom_call_target="tpu_custom_call" | custom-call | tf_op jit(solution)/shard_map/layer/pallas_call | solution.py:588
  87.5 2.0 %copy.12 = bf16[4,640,128]{2,1,0:T(8,128)(2,1)} copy(bf16[4,640,128]{2,1,0:T(8,128)(2,1)} %layer.1) | data formatting | bytes 1310720

commit v4 on v3

--- a/solution.py
+++ b/solution.py
@@ -21,29 +21,29 @@
 N_SEM = 192
 
 SCHEDULE = (
-    "pre0 pre2 pre4 pre6",
-    "enter u0:0 wo:0 look",
-    "pre1 pre3 u1:0 pre5",
-    "pre7 d2:0 wo:1 u0:1",
-    "turns summary near20 d1:0",
-    "wo:2 near21 near10 near11",
-    "u1:1 d2:1 d3:0 wo:3",
-    "memory u0:2 near30 d0:0",
-    "near31 d1:1 near01 u1:2",
-    "d3:1 bank_b d2:2 near00",
-    "u0:3 d0:1 d1:2 bank_c",
-    "far200 far210 far100 far110",
-    "u1:3 far300 far310 far010",
-    "d3:2 far000 d2:3 far201",
+    "pre0 pre2 enter u0:0",
+    "u1:0 pre4 wo:0 pre6",
+    "d2:0 look pre1 d1:0",
+    "pre3 d3:0 u0:1 wo:1",
+    "u1:1 d0:0 pre5 pre7",
+    "wo:2 turns summary d2:1",
+    "d1:1 d3:1 near20 u0:2",
+    "near21 near10 u1:2 d0:1",
+    "near11 wo:3 memory near30",
+    "near31 d2:2 near01 d1:2",
+    "d3:2 u0:3 u1:3 bank_b",
+    "near00 d0:2 d2:3 d1:3",
+    "d3:3 bank_c far200 far210",
+    "far100 far110 u0:4 far300",
+    "far310 far010 far000 far201",
     "far211 far101 far111 far301",
-    "far311 far011 far001 u0:4",
-    "d0:2 d1:3 mix0 norm0",
-    "u1:4 up000 up010 d3:3",
+    "far311 far011 far001 u1:4",
+    "d0:3 d2:4 d1:4 mix0",
+    "d3:4 norm0 up000 up010",
     "u0:5 up020 up030 up100",
-    "d2:4 up110 u1:5 up120",
-    "d0:3 up130 d2:5 down20",
-    "d1:4 d1:5 down10 d3:4",
-    "d3:5 down30 d0:4 d0:5",
+    "up110 d0:4 u1:5 up120",
+    "up130 d2:5 down20 d1:5",
+    "down10 d3:5 down30 d0:5",
     "down00 mix1 norm1 up001",
     "up011 up021 up031 up101",
     "up111 up121 up131 down21",

time: 89.9 us -> 94.6 us (1.052)
  Pallas kernels: 87.5 us -> 92.5 us
    pallas_call x1, Pallas kernels: 87.5 us -> 92.5 us  [body(): pl.pallas_call(kernel, name='layer', out_shape=jax.ShapeDtypeStruct((fram...]
where the time goes in v4:
time: 94.6 us; the launch traced here: 94.4 us
  Pallas kernels  92.5 us (98%)
  local copies, waits for them, and re-layouts  1.97 us (2%)
    pallas_call x1, Pallas kernels, body(): pl.pallas_call(kernel, name='layer', out_shape=jax.ShapeDtypeStruct((fram...  92.5 us
    unnamed x1, local copies, waits for them, and re-layouts  1.97 us

profile of v4, /device:TPU:1, one launch (start us, length us, event | category | flops | bytes accessed | tf_op | source)
XLA Modules:
  0.0 94.4 jit_solution(1883503412133195272)
XLA Ops:
  0.0 92.5 %layer.1 = bf16[4,640,128]{2,1,0:T(8,128)(2,1)} custom-call(s32[4]{0:T(128)} %valid.1, f32[1,1024]{1,0:T(1,128)} %bitcast.2, f32[1,1024]{1,0:T(1,128)} %bitcast.3, bf16[4,640,1024]{2,1,0:T(8,128)(2,1)} %frames.1, bf16[1024,128]{1,0:T(8,128)(2,1)} %wq.1, bf16[1024,128]{1,0:T(8,128)(2,1)} %wk.1, bf16[1024,128]{1,0:T(8,128)(2,1)} %wv.1, bf16[128,1024]{1,0:T(8,128)(2,1)} %wo.1, ...), custom_call_target="tpu_custom_call" | custom-call | tf_op jit(solution)/shard_map/layer/pallas_call | solution.py:588
  92.5 2.0 %copy.12 = bf16[4,640,128]{2,1,0:T(8,128)(2,1)} copy(bf16[4,640,128]{2,1,0:T(8,128)(2,1)} %layer.1) | data formatting | bytes 1310720
